TPU v7x, 256 devices: a whole 4x4x8 slice. The times are simulated.
256 devices in a mesh: island: 16 (over y, z_lo), fsdp: 16 (over z_hi, x, core).
Axes of the slice: x: 4, y: 4, z: 8 (z_hi: 2, z_lo: 4; z = z_hi * 4 + z_lo), core: 2. Of those that a mesh axis runs over, the one named last changes fastest.
Arguments:
- acts: bfloat16 [131072, 832], P(('island', 'fsdp')), may hold values from -6 to 6
- grad_out: bfloat16 [131072, 4096], P(('island', 'fsdp')), may hold values from -6 to 6
- next_acts: bfloat16 [131072, 832], P(('island', 'fsdp')), may hold values from -6 to 6
- inner_params: float32 [16, 4096, 832], P('island', 'fsdp'), may hold values from -0.2 to 0.2
- adam_first: float32 [16, 4096, 832], P('island', 'fsdp'), may hold values from -0.06 to 0.06
- adam_second: float32 [16, 4096, 832], P('island', 'fsdp'), may hold values from 1e-06 to 0.001
- base_params: float32 [4096, 832], P('fsdp'), may hold values from -0.21875 to 0.21875
- outer_moment: float32 [4096, 832], P('fsdp'), may hold values from -0.06 to 0.06
Outputs:
- new_base: float32 [4096, 832], P('fsdp', 'island')
- new_moment: float32 [4096, 832], P('fsdp', 'island')
- next_out: bfloat16 [131072, 4096], P(('island', 'fsdp'))
All inputs are finite; a program needn't handle non-finite values.
Results may differ from a plain program's by a relative error of at most 0.005.
Values may be sent and summed in bfloat16 or wider, within the bound.
A program may use at most 128 MiB of HBM per device.

v0:
```python
import jax
import jax.numpy as jnp
from jax import lax
from jax.sharding import PartitionSpec as P

INNER_STEP = 500


def per_device(
    acts, grad_out, next_acts, inner_params, adam_first, adam_second, base_params, outer_moment
):
    groups = lax.axis_size("fsdp")
    replicas = lax.axis_size("island")
    rows = acts.shape[0] * groups
    summed = lax.psum_scatter(
        lax.dot_general(
            grad_out, acts, (((0,), (0,)), ((), ())), preferred_element_type=jnp.float32
        ),
        "fsdp",
        scatter_dimension=0,
        tiled=True,
    )
    grad = summed / rows
    corr_one = 1.0 - 0.9**INNER_STEP
    corr_two = 1.0 - 0.95**INNER_STEP
    moment_one = 0.9 * adam_first[0] + 0.1 * grad
    moment_two = 0.95 * adam_second[0] + 0.05 * grad * grad
    stepped = inner_params[0] - 0.02 * (moment_one / corr_one) / (
        jnp.sqrt(moment_two / corr_two) + 1e-08
    )
    delta = base_params - stepped
    width = base_params.shape[1] // replicas
    offset = lax.axis_index("island") * width
    mean_delta = lax.psum(delta, "island") / replicas
    new_moment = 0.9 * outer_moment + mean_delta
    new_base = base_params - 0.7 * (mean_delta + 0.9 * new_moment)
    fresh = new_base.astype(jnp.bfloat16)
    base_out = lax.dynamic_slice_in_dim(new_base, offset, width, 1)
    moment_out = lax.dynamic_slice_in_dim(new_moment, offset, width, 1)
    next_out = lax.dot_general(
        next_acts,
        lax.all_gather(fresh, "fsdp", axis=0, tiled=True),
        (((1,), (1,)), ((), ())),
        preferred_element_type=jnp.float32,
    )
    return (base_out, moment_out, next_out.astype(jnp.bfloat16))


def solution(mesh):
    in_specs = (
        P(("island", "fsdp"), None),
        P(("island", "fsdp"), None),
        P(("island", "fsdp"), None),
        P("island", "fsdp", None),
        P("island", "fsdp", None),
        P("island", "fsdp", None),
        P("fsdp", None),
        P("fsdp", None),
    )
    out_specs = (P("fsdp", "island"), P("fsdp", "island"), P(("island", "fsdp"), None))
    return jax.shard_map(
        per_device, mesh=mesh, in_specs=in_specs, out_specs=out_specs, check_vma=False
    )
```

profile of v0, /device:TPU:1, one launch (start us, length us, event | category | flops | bytes accessed | tf_op | source)
XLA Modules:
  0.0 490.0 jit_solution(7471986041213380416)
XLA Ops:
  7.2 0.0 copy-start
  7.2 0.0 reduce-scatter.2.cloned.1.call-start
  7.2 1.1 copy-done
  8.3 9.0 %fusion.8 = f32[4096,832]{0,1:T(8,128)} fusion(bf16[512,832]{0,1:T(8,128)(2,1)S(1)} %copy-done, bf16[512,4096]{1,0:T(8,128)(2,1)} %param.9), kind=kOutput, calls=%fused_computation.15 | convolution fusion | flops 3489660928 | bytes 18677760 | tf_op jit(solution)/shard_map/dot_general | solution.py:16
  17.3 0.0 copy-start.1
  17.3 0.0 copy-start.2
  17.3 0.0 copy-start.3
  17.3 0.0 reduce-scatter.2.cloned.1.call-update
  17.4 0.0 all-reduce.2.cloned.1.call-start
  17.4 185.6 %reduce-scatter.2.cloned.1.call-done = f32[256,832]{0,1:T(8,128)} async-done(((f32[4096,832]{0,1:T(8,128)}), f32[256,832]{0,1:T(8,128)}) %reduce-scatter.2.cloned.1.call-update) | async-done | bytes 851984 | tf_op jit(solution)/shard_map/reduce_scatter | solution.py:15
  203.0 0.0 copy-done.1
  203.0 0.0 copy-done.2
  203.0 0.0 copy-done.3
  203.0 2.9 fusion.5
  205.9 0.0 all-reduce.2.cloned.1.call-update
  206.0 0.0 all-gather.2.cloned.1.call-start
  206.0 150.0 %all-reduce.2.cloned.1.call-done = f32[256,832]{0,1:T(8,128)} async-done(((f32[256,832]{0,1:T(8,128)}), f32[256,832]{0,1:T(8,128)}) %all-reduce.2.cloned.1.call-update) | async-done | bytes 851984 | tf_op jit(solution)/shard_map/psum | solution.py:34
  356.0 2.4 fusion.7
  358.5 0.0 all-gather.2.cloned.1.call-update
  358.5 0.7 constant_dynamic-slice_fusion
  359.1 108.3 %all-gather.2.cloned.1.call-done = bf16[4096,832]{0,1:T(8,128)(2,1)} async-done(((bf16[256,832]{0,1:T(8,128)(2,1)}), bf16[4096,832]{0,1:T(8,128)(2,1)}) %all-gather.2.cloned.1.call-update) | async-done | bytes 6815760 | tf_op jit(solution)/shard_map/all_gather | solution.py:42
  467.4 9.8 %fusion = bf16[512,4096]{0,1:T(8,128)(2,1)} fusion(bf16[4096,832]{0,1:T(8,128)(2,1)} %all-gather.2.cloned.1.call-done, bf16[512,832]{0,1:T(8,128)(2,1)} %param.10), kind=kOutput, calls=%fused_computation.1 | convolution fusion | flops 3491758080 | bytes 11862016 | tf_op jit(solution)/shard_map/dot_general | solution.py:40
  477.2 6.3 %copy.11 = bf16[512,4096]{1,0:T(8,128)(2,1)} copy(bf16[512,4096]{0,1:T(8,128)(2,1)} %fusion) | data formatting | bytes 8388608
Async XLA Ops:
  7.2 1.2 copy-start
  7.2 195.8 %reduce-scatter.2.cloned.1.call-start = ((), (), s32[]{:S(2)}) async-start(), calls=%async_computation.1 | async-start | bytes 14483456 | tf_op jit(solution)/shard_map/reduce_scatter | solution.py:15
  17.3 185.7 %copy-start.1 = (f32[256,832]{0,1:T(8,128)S(1)}, f32[256,832]{0,1:T(8,128)}, u32[]{:S(2)}) copy-start(f32[256,832]{0,1:T(8,128)} %param.14) | copy-start | bytes 2555908
  17.3 185.7 %copy-start.2 = (f32[1,256,832]{1,2,0:T(8,128)S(1)}, f32[1,256,832]{1,2,0:T(8,128)}, u32[]{:S(2)}) copy-start(f32[1,256,832]{1,2,0:T(8,128)} %param.11) | copy-start | bytes 2555908
  17.3 185.7 %copy-start.3 = (f32[1,256,832]{1,2,0:T(8,128)S(1)}, f32[1,256,832]{1,2,0:T(8,128)}, u32[]{:S(2)}) copy-start(f32[1,256,832]{1,2,0:T(8,128)} %param.13) | copy-start | bytes 2555908
  17.4 338.7 %all-reduce.2.cloned.1.call-start = ((), (), s32[]{:S(2)}) async-start(), calls=%async_computation.2 | async-start | bytes 1703936 | tf_op jit(solution)/shard_map/psum | solution.py:34
  206.0 261.4 %all-gather.2.cloned.1.call-start = ((), (), s32[]{:S(2)}) async-start(), calls=%async_computation.3 | async-start | bytes 7241728 | tf_op jit(solution)/shard_map/all_gather | solution.py:42
Sparse Core Ops, SparseCore 0:
  17.5 185.4 reduce-scatter.1
  206.2 149.7 all-reduce.1
  359.5 107.8 all-gather.1
where the time goes:
time: 490 us
  waiting for transfers between devices  444 us (91%)
  matrix products  18.8 us (4%)
  between operations  13.8 us (3%)
  local copies, waits for them, and re-layouts  8.09 us (2%)
  other arithmetic  5.31 us (1%)
    reduce_scatter x1, waiting for transfers between devices, per_device(): lax.psum_scatter(lax.dot_general(grad_out, acts, (((0,), (0,)), ((), ()))...  186 us
    psum x1, waiting for transfers between devices, per_device(): mean_delta = lax.psum(delta, 'island') / replicas  150 us
    all_gather x1, waiting for transfers between devices, per_device(): lax.all_gather(fresh, 'fsdp', axis=0, tiled=True)  108 us
  transfers between devices with their start and end apart: 3, of which 3 were waited for; matrix products, arithmetic and copies ran while one was open for 0% of the time, Pallas kernels for 0%

commit v1 on v0

v1 whole, which is shorter than its diff:
```python
import jax
import jax.numpy as jnp
from jax import lax
from jax.experimental import pallas as pl
from jax.experimental.pallas import tpu as pltpu
from jax.sharding import PartitionSpec as P

INNER_STEP = 500
MESH = pl.DeviceIdType.MESH
BF = jnp.bfloat16
F32 = jnp.float32
CHUNKS = ((0, 208, 0, 128), (0, 208, 128, 128))
SPLIT = (False, True)
NB = 4
RB = 208
RELS = (2, 1, 3, 0)
N_SEND = 32


def comm_kernel(
    acts, gout, inner, mom1, mom2, base, omom, nacts,
    w_out, nb_out, nm_out, na_out,
    acts_t, g_v, part,
    s1, r1, s2, r2, s3, r3, s4, r4, s5, r5, r6,
    st_t, base_c, w_v, nb_v, nm_v, na_t, na_v,
    in_sem, gl_sem, gs_sem, gr_sem, bs_sem, br_sem, snd, rcv, out_sem,
):
    isl, fs = lax.axis_index("island"), lax.axis_index("fsdp")
    y, zl = isl // 4, lax.rem(isl, 4)
    zh, x, c = fs // 8, lax.rem(fs // 2, 4), lax.rem(fs, 2)
    z = zh * 4 + zl
    oc, ozh = 1 - c, 1 - zh

    def dev(dx=0, dy=0, dz=0, dc=0):
        nz = lax.rem(z + dz, 8)
        ny, nx, nc = lax.rem(y + dy, 4), lax.rem(x + dx, 4), lax.rem(c + dc, 2)
        return (ny * 4 + lax.rem(nz, 4), ((nz // 4) * 4 + nx) * 2 + nc)

    def remote(src, dst, ss, rs, to):
        return pltpu.make_async_remote_copy(
            src_ref=src, dst_ref=dst, send_sem=ss, recv_sem=rs, device_id=to, device_id_type=MESH
        )

    def col(rel, h, par):
        nx = lax.rem(x + rel, 4)
        return pl.ds(pl.multiple_of(((h * 4 + nx) * 2 + par) * 256, 256), 256)

    load_acts = pltpu.make_async_copy(acts, acts_t.at[0], in_sem.at[0])
    load_acts.start()
    loads = {}
    for n, rel in enumerate(RELS):
        for h in range(2):
            cp = pltpu.make_async_copy(
                gout.at[:, col(rel, h, c)], g_v.at[n, h, pl.ds(0, 512)], gl_sem.at[n * 2 + h]
            )
            cp.start()
            loads[n, h] = cp
    states = []
    for n, ref in enumerate((inner, mom1, mom2, base, omom, nacts)):
        cp = pltpu.make_async_copy(ref, st_t.at[n] if n < 5 else na_t, in_sem.at[1 + n])
        cp.start()
        states.append(cp)

    bar = pltpu.get_barrier_semaphore()
    peers = [dev(dc=1)] + [dev(dx=d) for d in (1, 2, 3)] + [dev(dy=d) for d in (1, 2, 3)]
    peers += [dev(dz=d) for d in range(1, 8)]
    for p in peers:
        pl.semaphore_signal(bar, inc=1, device_id=p, device_id_type=MESH)
    pl.semaphore_wait(bar, len(peers))

    swap_acts = remote(acts, acts_t.at[1], gs_sem.at[8], gr_sem.at[8], dev(dc=1))
    swap_acts.start()
    swaps = {}
    for n, rel in enumerate(RELS):
        for h in range(2):
            cp = remote(
                gout.at[:, col(rel, h, oc)], g_v.at[n, h, pl.ds(512, 512)],
                gs_sem.at[n * 2 + h], gr_sem.at[n * 2 + h], dev(dc=1),
            )
            cp.start()
            swaps[n, h] = cp

    load_acts.wait()
    swap_acts.wait_recv()

    def multiply(n, h, put):
        loads[n, h].wait()
        swaps[n, h].wait_recv()

        def body(b, carry):
            total = jnp.dot(acts_t[0, b], g_v[n, h, :512], preferred_element_type=F32)
            total += jnp.dot(acts_t[1, b], g_v[n, h, 512:], preferred_element_type=F32)
            put(b, total)
            return carry

        lax.fori_loop(0, NB, body, 0)

    def to_bf(ref, h):
        def put(b, value):
            ref[h, b] = value.astype(BF)
        return put

    def to_part(k):
        def put(b, value):
            part[k, b] = value
        return put

    pending = []

    def start(k, slot, src, dst, to):
        cp = remote(src, dst, snd.at[k, slot], rcv.at[k, slot], to)
        cp.start()
        pending.append(cp)
        return cp

    live = {}

    def cut(k):
        r0, rn, l0, ln = CHUNKS[k]
        return pl.ds(r0, rn), pl.ds(l0, ln)

    def t1(k):
        rows, lanes = cut(k)
        for h in range(2):
            live["t1", k, h] = start(
                k, h, s1.at[h, :, rows, lanes], r1.at[h, :, rows, lanes], dev(dx=1 if h == 0 else 3)
            )

    def t2(k):
        rows, lanes = cut(k)
        for h in range(2):
            live["t2", k, h] = start(
                k, 2 + h, s2.at[h, :, rows, lanes], r2.at[h, :, rows, lanes], dev(dx=3 if h == 0 else 1)
            )

    def t3(k):
        rows, lanes = cut(k)
        for h in range(2):
            live["t1", k, h].wait_recv()

            def body(b, carry):
                s3[h, b, rows, lanes] = (
                    part[h, b, rows, lanes] + r1[h, b, rows, lanes].astype(F32)
                ).astype(BF)
                return carry

            lax.fori_loop(0, NB, body, 0)
            live["t3", k, h] = start(
                k, 4 + h, s3.at[h, :, rows, lanes], r3.at[h, :, rows, lanes], dev(dx=1 if h == 0 else 3)
            )

    def t4(k):
        rows, lanes = cut(k)
        for h in range(2):
            live["t2", k, h].wait_recv()
            live["t3", k, h].wait_recv()

        def body(b, carry):
            s4[b, rows, lanes] = (
                part[2 + ozh, b, rows, lanes]
                + r2[ozh, b, rows, lanes].astype(F32)
                + r3[ozh, b, rows, lanes].astype(F32)
            ).astype(BF)
            return carry

        lax.fori_loop(0, NB, body, 0)
        live["t4", k] = start(k, 6, s4.at[:, rows, lanes], r4.at[:, rows, lanes], dev(dz=4))

    corr_one = 1.0 - 0.9**INNER_STEP
    corr_two = 1.0 - 0.95**INNER_STEP

    def t5(k):
        rows, lanes = cut(k)
        live["t4", k].wait_recv()

        def body(b, carry):
            grad = (
                part[2 + zh, b, rows, lanes]
                + r2[zh, b, rows, lanes].astype(F32)
                + r3[zh, b, rows, lanes].astype(F32)
                + r4[b, rows, lanes].astype(F32)
            ) * (1.0 / 8192.0)
            one = 0.9 * st_t[1, b, rows, lanes] + 0.1 * grad
            two = 0.95 * st_t[2, b, rows, lanes] + 0.05 * grad * grad
            step = (one * (0.02 / corr_one)) / (jnp.sqrt(two * (1.0 / corr_two)) + 1e-08)
            s5[b, rows, lanes] = st_t[3, b, rows, lanes] - (st_t[0, b, rows, lanes] - step)
            return carry

        lax.fori_loop(0, NB, body, 0)
        for d in (1, 2, 3):
            live["t5", k, d] = start(
                k, 6 + d, s5.at[lax.rem(y + d, 4), rows, lanes], r5.at[d - 1, rows, lanes], dev(dy=d)
            )

    def t6(k):
        rows, lanes = cut(k)
        for d in (1, 2, 3):
            live["t5", k, d].wait_recv()
        total = s5[y, rows, lanes]
        for d in range(3):
            total += r5[d, rows, lanes]
        r6[z, rows, lanes] = total.astype(BF)
        for d in range(1, 8):
            live["t6", k, d] = start(
                k, 9 + d, r6.at[z, rows, lanes], r6.at[z, rows, lanes], dev(dz=d)
            )

    def t7(k):
        rows, lanes = cut(k)
        for d in range(1, 8):
            live["t6", k, d].wait_recv()
        if k == 0:
            live["base"].wait_recv()

        def mean(h):
            total = r6[4 * h, rows, lanes].astype(F32)
            for m in range(1, 4):
                total += r6[4 * h + m, rows, lanes].astype(F32)
            return total * (1.0 / 16.0)

        for h in range(2):
            w_v[c, h, x, y, rows, lanes] = (base_c[h, rows, lanes] - 1.33 * mean(h)).astype(BF)
        own = mean(zh)
        nb_v[rows, lanes] = base_c[zh, rows, lanes] - 1.33 * own
        nm_v[rows, lanes] = 0.9 * st_t[4, y, rows, lanes] + own
        if SPLIT[k]:
            for d in (1, 2, 3):
                ref = w_v.at[c, 0, x, y, rows, lanes]
                live["t7", k, 0, d] = start(k, 16 + d, ref, ref, dev(dx=d))
                ref = w_v.at[c, 1, x, y, rows, lanes]
                live["t7", k, 1, d] = start(k, 19 + d, ref, ref, dev(dy=d))
        else:
            for d in (1, 2, 3):
                ref = w_v.at[c, :, x, y, rows, lanes]
                live["t7", k, 0, d] = start(k, 16 + d, ref, ref, dev(dx=d))

    def to_core(k, slot, ref):
        live["core", k, slot] = start(k, slot, ref, ref, dev(dc=1))

    def t8(k):
        rows, lanes = cut(k)
        if SPLIT[k]:
            for h in range(2):
                for d in (1, 2, 3):
                    live["t7", k, h, d].wait_recv()
                ref = w_v.at[c, 0, :, y, rows, lanes] if h == 0 else w_v.at[c, 1, x, :, rows, lanes]
                for d in (1, 2, 3):
                    to = dev(dy=d) if h == 0 else dev(dx=d)
                    live["t8", k, h, d] = start(k, 22 + 3 * h + d, ref, ref, to)
                to_core(k, 29 + h, ref)
        else:
            for d in (1, 2, 3):
                live["t7", k, 0, d].wait_recv()
            ref = w_v.at[c, :, :, y, rows, lanes]
            for d in (1, 2, 3):
                live["t8", k, 0, d] = start(k, 22 + d, ref, ref, dev(dy=d))
            to_core(k, 29, ref)

    def t9(k):
        rows, lanes = cut(k)
        for d in (1, 3, 2):
            if SPLIT[k]:
                for h in range(2):
                    live["t8", k, h, d].wait_recv()
                    ref = (
                        w_v.at[c, 0, :, lax.rem(y + 4 - d, 4), rows, lanes]
                        if h == 0
                        else w_v.at[c, 1, lax.rem(x + 4 - d, 4), :, rows, lanes]
                    )
                    to_core(k, 30 + h * 3 + d, ref)
            else:
                live["t8", k, 0, d].wait_recv()
                to_core(k, 30 + d, w_v.at[c, :, :, lax.rem(y + 4 - d, 4), rows, lanes])

    outs = []

    def t10(k):
        rows, lanes = cut(k)
        for key, cp in live.items():
            if key[0] == "core" and key[1] == k:
                cp.wait_recv()
        for p in range(2):
            for h in range(2):
                cp = pltpu.make_async_copy(
                    w_v.at[p, h, :, :, rows, lanes], w_out.at[p, h, :, :, rows, lanes],
                    out_sem.at[k * 4 + p * 2 + h],
                )
                cp.start()
                outs.append(cp)

    def stage_mul():
        multiply(0, 0, to_bf(s1, 0))
        multiply(0, 1, to_bf(s1, 1))
        t1(0)
        multiply(1, 1, to_bf(s2, 1))
        multiply(2, 0, to_bf(s2, 0))
        t2(0)
        t1(1)
        multiply(1, 0, to_part(0))
        multiply(2, 1, to_part(1))
        multiply(3, 0, to_part(2))
        multiply(3, 1, to_part(3))

    def stage_base():
        states[3].wait()
        states[4].wait()
        base_c[zh] = st_t[3, y] - 0.567 * st_t[4, y]
        live["base"] = remote(base_c.at[zh], base_c.at[zh], bs_sem, br_sem, dev(dz=4))
        live["base"].start()
        pending.append(live["base"])

    def stage_rest():
        for n in (0, 1, 2, 5):
            states[n].wait()
        na_v[...] = na_t[...].T
        cp = pltpu.make_async_copy(na_v, na_out, out_sem.at[4 * len(CHUNKS) + 2])
        cp.start()
        outs.append(cp)

    steps = [
        (stage_mul,), (stage_base,), (t3, 0), (t2, 1), (stage_rest,), (t4, 0), (t3, 1), (t5, 0), (t4, 1),
        (t6, 0), (t7, 0), (t5, 1), (t8, 0), (t6, 1), (t9, 0), (t7, 1), (t10, 0), (t8, 1), (t9, 1), (t10, 1),
    ]
    for step in steps:
        step[0](*step[1:])
    for n, (src, dst) in enumerate(((nb_v, nb_out), (nm_v, nm_out))):
        cp = pltpu.make_async_copy(src, dst, out_sem.at[4 * len(CHUNKS) + n])
        cp.start()
        outs.append(cp)
    swap_acts.wait_send()
    for cp in swaps.values():
        cp.wait_send()
    for cp in pending:
        cp.wait_send()
    for cp in outs:
        cp.wait()


def project_kernel(a_ref, w_ref, nb_ref, nm_ref, o_ref, nbo_ref, nmo_ref):
    o_ref[...] = jnp.dot(
        a_ref[...], w_ref[...].reshape(NB * RB, 256), preferred_element_type=F32
    ).astype(BF)
    zl = lax.rem(lax.axis_index("island"), 4)

    @pl.when(pl.program_id(0) == 0)
    def _():
        for k in range(4):
            @pl.when(zl == k)
            def _():
                nbo_ref[...] = nb_ref[pl.ds(52 * k, 52), :]
                nmo_ref[...] = nm_ref[pl.ds(52 * k, 52), :]


def per_device(
    acts, grad_out, next_acts, inner_params, adam_first, adam_second, base_params, outer_moment
):
    n = len(CHUNKS)
    dma, vm = pltpu.SemaphoreType.DMA, pltpu.VMEM
    hbm = pl.BlockSpec(memory_space=pl.ANY)
    block = (NB, RB, 256)
    acts_tr = acts.T.reshape(NB, RB, 512)
    states = [a[0].T.reshape(block) for a in (inner_params, adam_first, adam_second)]
    states += [a.T.reshape(block) for a in (base_params, outer_moment)]
    w, nb, nm, na = pl.pallas_call(
        comm_kernel,
        out_shape=(
            jax.ShapeDtypeStruct((2, 2, 4) + block, BF),
            jax.ShapeDtypeStruct((RB, 256), F32),
            jax.ShapeDtypeStruct((RB, 256), F32),
            jax.ShapeDtypeStruct((512, 832), BF),
        ),
        in_specs=[hbm] * 8,
        out_specs=(hbm,) * 4,
        scratch_shapes=[
            vm((2, NB, RB, 512), BF), vm((4, 2, 1024, 256), BF),
            vm((4,) + block, F32),
            vm((2,) + block, BF), vm((2,) + block, BF), vm((2,) + block, BF), vm((2,) + block, BF),
            vm((2,) + block, BF), vm((2,) + block, BF), vm(block, BF), vm(block, BF), vm(block, F32),
            vm((3, RB, 256), F32), vm((8, RB, 256), BF),
            vm((5,) + block, F32), vm((2, RB, 256), F32),
            vm((2, 2, 4) + block, BF), vm((RB, 256), F32), vm((RB, 256), F32),
            vm((832, 512), BF), vm((512, 832), BF),
            dma((7,)), dma((8,)), dma((9,)), dma((9,)), dma, dma,
            dma((n, 40)), dma((n, 40)), dma((4 * n + 3,)),
        ],
        compiler_params=pltpu.CompilerParams(
            collective_id=0, has_side_effects=True, vmem_limit_bytes=60 * 2**20
        ),
        name="outer_round",
    )(acts_tr, grad_out, *states, next_acts.T)
    whole = pl.BlockSpec((RB, 256), lambda i: (0, 0))
    small = pl.BlockSpec((52, 256), lambda i: (0, 0))
    next_out, base_out, moment_out = pl.pallas_call(
        project_kernel,
        grid=(16,),
        out_shape=(
            jax.ShapeDtypeStruct((512, 4096), BF),
            jax.ShapeDtypeStruct((52, 256), F32),
            jax.ShapeDtypeStruct((52, 256), F32),
        ),
        in_specs=[
            pl.BlockSpec((512, 832), lambda i: (0, 0)),
            pl.BlockSpec((None, None, None) + block, lambda i: (i % 2, i // 8, (i // 2) % 4, 0, 0, 0)),
            whole,
            whole,
        ],
        out_specs=(pl.BlockSpec((512, 256), lambda i: (0, i)), small, small),
        compiler_params=pltpu.CompilerParams(vmem_limit_bytes=60 * 2**20),
        name="project",
    )(na, w, nb, nm)
    return base_out.T, moment_out.T, next_out


def solution(mesh):
    in_specs = (
        P(("island", "fsdp"), None),
        P(("island", "fsdp"), None),
        P(("island", "fsdp"), None),
        P("island", "fsdp", None),
        P("island", "fsdp", None),
        P("island", "fsdp", None),
        P("fsdp", None),
        P("fsdp", None),
    )
    out_specs = (P("fsdp", "island"), P("fsdp", "island"), P(("island", "fsdp"), None))
    return jax.shard_map(
        per_device, mesh=mesh, in_specs=in_specs, out_specs=out_specs, check_vma=False
    )
```

time: 490 us -> 137 us (0.28)
  waiting for transfers between devices: 444 us -> 0 us
  Pallas kernels: 0 us -> 136 us
  matrix products: 18.8 us -> 0 us
  between operations: 13.8 us -> 0.64 us
  local copies, waits for them, and re-layouts: 8.09 us -> 0 us
  other arithmetic: 5.31 us -> 0 us
    reduce_scatter x1 -> x0, waiting for transfers between devices: 186 us -> none  [per_device(): lax.psum_scatter(lax.dot_general(grad_out, acts, (((0,), (0,)), ((), ()))...]
    psum x1 -> x0, waiting for transfers between devices: 150 us -> none  [per_device(): mean_delta = lax.psum(delta, 'island') / replicas]
    pallas_call x0 -> x2, Pallas kernels: none -> 136 us  [the longest x1 122 us: per_device(): pl.pallas_call(comm_kernel, out_shape=(jax.ShapeDtypeStruct((2, 2, 4) + b...]
    all_gather x1 -> x0, waiting for transfers between devices: 108 us -> none  [per_device(): lax.all_gather(fresh, 'fsdp', axis=0, tiled=True)]
    dot_general x2 -> x0, matrix products: 18.8 us -> none  [the longest x1 9.75 us: per_device(): lax.dot_general(next_acts, lax.all_gather(fresh, 'fsdp', axis=0, tiled=Tr...]
    unnamed x9 -> x0, local copies, waits for them, and re-layouts: 7.43 us -> none
  transfers between devices with their start and end apart: 3 -> 0, of which waited for: 3 -> 0; matrix products, arithmetic and copies ran while one was open for 0% -> 0% of each run, Pallas kernels for 0% -> 0%
where the time goes in v1:
time: 137 us
  Pallas kernels  136 us (99%)
    pallas_call x1, Pallas kernels, per_device(): pl.pallas_call(comm_kernel, out_shape=(jax.ShapeDtypeStruct((2, 2, 4) + b...  122 us
    pallas_call x1, Pallas kernels, per_device(): pl.pallas_call(project_kernel, grid=(16,), out_shape=(jax.ShapeDtypeStruc...  14.4 us

profile of v1, /device:TPU:1, one launch (start us, length us, event | category | flops | bytes accessed | tf_op | source)
XLA Modules:
  0.0 136.7 jit_solution(10522167448503100716)
XLA Ops:
  0.6 121.6 %outer_round.1 = (bf16[2,2,4,4,208,256]{5,4,3,2,1,0:T(8,128)(2,1)}, f32[208,256]{1,0:T(8,128)}, f32[208,256]{1,0:T(8,128)}, bf16[512,832]{1,0:T(8,128)(2,1)}) custom-call(bf16[4,208,512]{2,1,0:T(8,128)(2,1)} %bitcast.27, bf16[512,4096]{1,0:T(8,128)(2,1)} %gout.1, f32[4,208,256]{2,1,0:T(8,128)} %bitcast.28, f32[4,208,256]{2,1,0:T(8,128)} %bitcast.29, ...), custom_call_target="tpu_custom_call" | custom-call | tf_op jit(solution)/shard_map/outer_round/pallas_call | solution.py:364
  122.3 14.4 %project.1 = (bf16[512,4096]{1,0:T(8,128)(2,1)}, f32[52,256]{1,0:T(8,128)}, f32[52,256]{1,0:T(8,128)}) custom-call(bf16[512,832]{1,0:T(8,128)(2,1)} %get-tuple-element.10.a_ref, bf16[2,2,4,4,208,256]{5,4,3,2,1,0:T(8,128)(2,1)} %get-tuple-element.11.w_ref, f32[208,256]{1,0:T(8,128)} %get-tuple-element.12.nb_ref, f32[208,256]{1,0:T(8,128)} %get-tuple-element.13.nm_ref), custom_call_target="tpu_custom_call" | custom-call | tf_op jit(solution)/shard_map/project/pallas_call | solution.py:393

commit v2 on v1

v2 whole, which is shorter than its diff:
```python
import jax
import jax.numpy as jnp
from jax import lax
from jax.experimental import pallas as pl
from jax.experimental.pallas import tpu as pltpu
from jax.sharding import PartitionSpec as P

INNER_STEP = 500
MESH = pl.DeviceIdType.MESH
BF = jnp.bfloat16
F32 = jnp.float32
CHUNKS = (
    (0, 48, 0, 128), (48, 64, 0, 128), (112, 96, 0, 128), (0, 96, 128, 128), (96, 64, 128, 128), (160, 48, 128, 128)
)
FIRST = (32, 32, 48, 48, 32, 32)
WIDE = (4, 5)
DIRECT = (10, 9, 11, 6, 14, 2, 8, 5, 7, 13, 15, 1, 3, 4, 12)
WIDE_ROWS, WIDE_LANES = pl.ds(96, 112), pl.ds(128, 128)
NB = 4
RB = 208
RELS = (2, 1, 3, 0)


def comm_kernel(
    acts, gout, inner, mom1, mom2, base, omom, nacts,
    w_v, nb_v, nm_v, na_v, half_v,
    acts_t, g_v, xs, xr, part,
    s1, r1, s2, r2, s3, r3, s4, r4, s5, r5, r6,
    st_t, na_t, base_c,
    in_sem, gl_sem, xs_sem, xr_sem, bs_sem, br_sem, snd, rcv,
):
    isl, fs = lax.axis_index("island"), lax.axis_index("fsdp")
    y, zl = isl // 4, lax.rem(isl, 4)
    zh, x, c = fs // 8, lax.rem(fs // 2, 4), lax.rem(fs, 2)
    oc, ozh = 1 - c, 1 - zh

    def dev(dx=0, dy=0, dl=0, dh=0, dc=0):
        ny, nl = lax.rem(y + dy, 4), lax.rem(zl + dl, 4)
        nh, nx, nc = lax.rem(zh + dh, 2), lax.rem(x + dx, 4), lax.rem(c + dc, 2)
        return (ny * 4 + nl, (nh * 4 + nx) * 2 + nc)

    def remote(src, dst, ss, rs, to):
        return pltpu.make_async_remote_copy(
            src_ref=src, dst_ref=dst, send_sem=ss, recv_sem=rs, device_id=to, device_id_type=MESH
        )

    def col(rel, h, par):
        nx = lax.rem(x + rel, 4)
        return pl.ds(pl.multiple_of(((h * 4 + nx) * 2 + par) * 256, 256), 256)

    loads = {}

    def load(n):
        for side, par in enumerate((oc, c)):
            for h in range(2):
                loads[n, side, h] = pltpu.make_async_copy(
                    gout.at[:, col(RELS[n], h, par)], g_v.at[n, side, h], gl_sem.at[n, side, h]
                )
                loads[n, side, h].start()

    load_acts = pltpu.make_async_copy(acts, acts_t, in_sem.at[0])
    load_acts.start()
    load(0)

    bar = pltpu.get_barrier_semaphore()
    peers = [dev(dc=1)] + [dev(dl=d, dh=1) for d in range(4)]
    peers += [dev(dx=d % 4, dy=d // 4) for d in range(1, 16)] + [dev(dl=d) for d in (1, 2, 3)]
    for p in peers:
        pl.semaphore_signal(bar, inc=1, device_id=p, device_id_type=MESH)
    load(1)

    states = []

    def load_states():
        for n, ref in enumerate((inner, mom1, mom2, base, omom, nacts)):
            cp = pltpu.make_async_copy(ref, st_t.at[n] if n < 5 else na_t, in_sem.at[1 + n])
            cp.start()
            states.append(cp)

    swaps = {}

    def give_mul(n, h):
        loads[n, 0, h].wait()
        value = jnp.dot(acts_t[...].reshape(NB * RB, 512), g_v[n, 0, h], preferred_element_type=F32)
        xs[n, h] = value.astype(BF).reshape(NB, RB, 256)

    def give_send(n, h, q=None):
        lanes = pl.ds(0, 256) if q is None else pl.ds(q * 128, 128)
        m = q or 0
        swaps[n, h, q] = remote(
            xs.at[n, h, :, :, lanes], xr.at[n, h, :, :, lanes], xs_sem.at[n, h, m], xr_sem.at[n, h, m], dev(dc=1)
        )
        swaps[n, h, q].start()

    def keep(n, h, ref, q=None):
        swaps[n, h, q].wait_recv()
        lanes = pl.ds(0, 256) if q is None else pl.ds(q * 128, 128)
        if (n, h) not in kept:
            loads[n, 1, h].wait()
            kept.add((n, h))

        value = jnp.dot(
            acts_t[...].reshape(NB * RB, 512), g_v[n, 1, h, :, lanes], preferred_element_type=F32
        )
        value = value.reshape(NB, RB, value.shape[1]) + xr[n, h, :, :, lanes].astype(F32)
        ref[:, :, lanes] = value.astype(ref.dtype)

    kept = set()
    pending = []

    def start(k, slot, src, dst, to):
        cp = remote(src, dst, snd.at[k, slot], rcv.at[k, slot], to)
        cp.start()
        pending.append(cp)
        return cp

    live = {}

    def cut(k):
        r0, rn, l0, ln = CHUNKS[k]
        return pl.ds(r0, rn), pl.ds(l0, ln)

    def t1(k, halves=(0, 1)):
        rows, lanes = cut(k)
        for h in halves:
            live["t1", k, h] = start(
                k, h, s1.at[h, :, rows, lanes], r1.at[h, :, rows, lanes], dev(dx=1 if h == 0 else 3)
            )

    def t2(k):
        rows, lanes = cut(k)
        for h in range(2):
            live["t2", k, h] = start(
                k, 2 + h, s2.at[h, :, rows, lanes], r2.at[h, :, rows, lanes], dev(dx=3 if h == 0 else 1)
            )

    def t3(k):
        rows, lanes = cut(k)
        for h in range(2):
            live["t1", k, h].wait_recv()

            def body(b, carry):
                s3[h, b, rows, lanes] = (
                    part[h, b, rows, lanes] + r1[h, b, rows, lanes].astype(F32)
                ).astype(BF)
                return carry

            lax.fori_loop(0, NB, body, 0)
            live["t3", k, h] = start(
                k, 4 + h, s3.at[h, :, rows, lanes], r3.at[h, :, rows, lanes], dev(dx=1 if h == 0 else 3)
            )

    def t4(k):
        rows, lanes = cut(k)
        for h in range(2):
            live["t2", k, h].wait_recv()
            live["t3", k, h].wait_recv()

        def body(b, carry):
            s4[b, rows, lanes] = (
                part[2 + ozh, b, rows, lanes]
                + r2[ozh, b, rows, lanes].astype(F32)
                + r3[ozh, b, rows, lanes].astype(F32)
            ).astype(BF)
            return carry

        lax.fori_loop(0, NB, body, 0)
        live["t4", k] = start(k, 6, s4.at[:, rows, lanes], r4.at[:, rows, lanes], dev(dh=1))

    corr_one = 1.0 - 0.9**INNER_STEP
    corr_two = 1.0 - 0.95**INNER_STEP

    def t5(k):
        rows, lanes = cut(k)
        live["t4", k].wait_recv()

        def body(b, carry):
            grad = (
                part[2 + zh, b, rows, lanes]
                + r2[zh, b, rows, lanes].astype(F32)
                + r3[zh, b, rows, lanes].astype(F32)
                + r4[b, rows, lanes].astype(F32)
            ) * (1.0 / 8192.0)
            one = 0.9 * st_t[1, b, rows, lanes] + 0.1 * grad
            two = 0.95 * st_t[2, b, rows, lanes] + 0.05 * grad * grad
            step = (one * (0.02 / corr_one)) / (jnp.sqrt(two * (1.0 / corr_two)) + 1e-08)
            s5[b, rows, lanes] = st_t[3, b, rows, lanes] - (st_t[0, b, rows, lanes] - step)
            return carry

        lax.fori_loop(0, NB, body, 0)
        for d in (1, 2, 3):
            live["t5", k, d] = start(
                k, 6 + d, s5.at[lax.rem(y + d, 4), rows, lanes], r5.at[d - 1, rows, lanes], dev(dy=d)
            )

    def t6(k):
        rows, lanes = cut(k)
        for d in (1, 2, 3):
            live["t5", k, d].wait_recv()
        total = s5[y, rows, lanes]
        for d in range(3):
            total += r5[d, rows, lanes]
        slot = zh * 4 + zl
        r6[slot, rows, lanes] = total.astype(BF)
        ref = r6.at[slot, rows, lanes]
        for d in (1, 2, 3):
            live["t6", k, d] = start(k, 9 + d, ref, ref, dev(dl=d))
        if k in WIDE:
            for d in range(4):
                live["t6", k, 4 + d] = start(k, 40 + d, ref, ref, dev(dl=d, dh=1))

    def parts_of(k):
        r0, rn, l0, ln = CHUNKS[k]
        return (pl.ds(r0, FIRST[k]), pl.ds(r0 + FIRST[k], rn - FIRST[k])), pl.ds(l0, ln)

    def gather_one(k, other):
        (first, second), lanes = parts_of(k)
        h = ozh if other else zh
        for d in (1, 2, 3):
            ref = w_v.at[c, h, x, y, first, lanes]
            live["mid", k, other, 0, d] = start(k, 13 + 6 * other + d, ref, ref, dev(dx=d))
            ref = w_v.at[c, h, x, y, second, lanes]
            live["mid", k, other, 1, d] = start(k, 16 + 6 * other + d, ref, ref, dev(dy=d))

    def t7(k):
        rows, lanes = cut(k)
        for d in (1, 2, 3):
            live["t6", k, d].wait_recv()
        if k in WIDE:
            for d in range(4):
                live["t6", k, 4 + d].wait_recv()

        def average(h):
            total = r6[h * 4, rows, lanes].astype(F32)
            for m in range(1, 4):
                total += r6[h * 4 + m, rows, lanes].astype(F32)
            return total * (1.0 / 16.0)

        mean = average(zh)
        moment = 0.9 * st_t[4, y, rows, lanes] + mean
        fresh = st_t[3, y, rows, lanes] - 0.7 * (mean + 0.9 * moment)
        w_v[c, zh, x, y, rows, lanes] = fresh.astype(BF)
        if k in WIDE:
            if "base" in live:
                live.pop("base").wait_recv()
            w_v[c, ozh, x, y, rows, lanes] = (base_c[1, rows, lanes] - 1.33 * average(ozh)).astype(BF)
            ref = w_v.at[c, :, x, y, rows, lanes]
            for d in DIRECT:
                live["all", k, d] = start(k, 13 + d, ref, ref, dev(dx=d % 4, dy=d // 4))
        else:
            ref = w_v.at[c, zh, x, y, rows, lanes]
            live["t7", k] = start(k, 13, ref, ref, dev(dh=1))
            gather_one(k, 0)
        nb_v[rows, lanes] = fresh
        nm_v[rows, lanes] = moment

    def t7b(k):
        live["t7", k].wait_recv()
        gather_one(k, 1)

    def gather_two(k, other):
        (first, second), lanes = parts_of(k)
        h = ozh if other else zh
        for p in range(2):
            for d in (1, 2, 3):
                live["mid", k, other, p, d].wait_recv()
            ref = w_v.at[c, h, :, y, first, lanes] if p == 0 else w_v.at[c, h, x, :, second, lanes]
            for d in (1, 2, 3):
                live["end", k, other, p, d] = start(
                    k, 25 + 6 * other + 3 * p + d, ref, ref, dev(dy=d) if p == 0 else dev(dx=d)
                )

    def gather_three(k, other):
        rows, lanes = cut(k)
        for p in range(2):
            for d in (1, 2, 3):
                live["end", k, other, p, d].wait_recv()
        ref = w_v.at[c, ozh if other else zh, :, :, rows, lanes]
        live["core", k, other] = start(k, 38 + other, ref, ref, dev(dc=1))

    def gather_all(k):
        rows, lanes = cut(k)
        for d in DIRECT:
            live["all", k, d].wait_recv()
        ref = w_v.at[c, :, :, :, rows, lanes]
        live["core", k, 0] = start(k, 38, ref, ref, dev(dc=1))

    def t10(k):
        live["core", k, 0].wait_recv()
        if k not in WIDE:
            live["core", k, 1].wait_recv()

    def stage_mul():
        load_acts.wait()
        give_mul(0, 0)
        give_mul(0, 1)
        load(2)
        load(3)
        pl.semaphore_wait(bar, len(peers))
        give_send(0, 0, 0)
        give_send(0, 1, 0)
        load_states()
        give_mul(1, 1)
        give_mul(2, 0)
        keep(0, 0, s1.at[0], 0)
        t1(0, (0,))
        t1(1, (0,))
        keep(0, 1, s1.at[1], 0)
        t1(0, (1,))
        t1(1, (1,))
        give_send(0, 0, 1)
        give_send(0, 1, 1)
        give_send(1, 1)
        give_send(2, 0)
        give_mul(1, 0)
        give_mul(2, 1)
        keep(1, 1, s2.at[1])
        keep(2, 0, s2.at[0])
        t2(0)
        give_send(1, 0)
        give_send(2, 1)
        keep(0, 0, s1.at[0], 1)
        keep(0, 1, s1.at[1], 1)
        for n, h in ((3, 0), (3, 1)):
            give_mul(n, h)
            give_send(n, h)
        for m, (n, h) in enumerate(((1, 0), (2, 1), (3, 0), (3, 1))):
            keep(n, h, part.at[m])

    def stage_rest():
        for cp in states:
            cp.wait()
        mine = st_t[3, y, WIDE_ROWS, WIDE_LANES] - 0.567 * st_t[4, y, WIDE_ROWS, WIDE_LANES]
        base_c[0, WIDE_ROWS, WIDE_LANES] = mine
        live["base"] = remote(
            base_c.at[0, WIDE_ROWS, WIDE_LANES], base_c.at[1, WIDE_ROWS, WIDE_LANES], bs_sem, br_sem, dev(dh=1)
        )
        live["base"].start()
        pending.append(live["base"])
        na_v[...] = na_t[...].T

    def product(p, hh):
        for xx in range(0, 4, 2):
            pair = jnp.concatenate(
                [w_v[p, hh, xx + m, :, :, :128].reshape(NB * RB, 128) for m in range(2)], axis=1
            )
            half_v[p, hh, xx // 2] = jnp.dot(na_v[...], pair, preferred_element_type=F32).astype(BF)

    done = []

    def drain(keep_last):
        n = len(pending) - keep_last
        for cp in pending[len(done) : n]:
            cp.wait_send()
            done.append(cp)

    steps = [
        (stage_mul,), (t2, 1), (t3, 0), (t3, 1), (t1, 2), (t2, 2), (t4, 0), (t4, 1), (t3, 2), (t1, 3),
        (stage_rest,), (t5, 0), (t2, 3), (t4, 2), (t5, 1), (t3, 3), (t6, 0), (t1, 5), (t2, 5), (t2, 4), (t6, 1),
        (t4, 3), (t3, 5), (t1, 4), (t5, 2), (t7, 0), (drain, 40), (t4, 5), (t3, 4), (t7, 1), (t6, 2), (t5, 3),
        (t7b, 0), (t4, 4), (gather_two, 0, 0), (t5, 5), (t7b, 1), (gather_two, 1, 0), (t6, 3), (t7, 2),
        (drain, 40), (gather_two, 0, 1), (t6, 5), (gather_three, 0, 0), (t5, 4), (gather_two, 1, 1),
        (gather_three, 1, 0), (t7, 3), (gather_two, 2, 0), (t6, 4), (t7b, 2), (gather_two, 3, 0), (t7, 5),
        (drain, 60), (gather_three, 1, 1), (t7b, 3), (gather_two, 2, 1), (t7, 4), (drain, 60),
        (gather_three, 0, 1), (gather_all, 5), (gather_two, 3, 1), (gather_three, 2, 1), (gather_three, 2, 0),
        (t10, 1), (t10, 0), (gather_three, 3, 0), (gather_all, 4), (t10, 5), (t10, 2), (gather_three, 3, 1),
        (product, 0, 1), (product, 1, 0), (product, 0, 0), (t10, 4), (product, 1, 1), (t10, 3),
    ]
    for step in steps:
        step[0](*step[1:])
    for cp in swaps.values():
        cp.wait_send()
    drain(0)


def project_kernel(a_ref, w_ref, nb_ref, nm_ref, half_ref, o_ref, nbo_ref, nmo_ref):
    step = pl.program_id(0)
    hh, pr = step // 2, lax.rem(step, 2)
    for p in range(2):
        pair = jnp.concatenate(
            [w_ref[p, hh, pr * 2 + m, :, :, 128:].reshape(NB * RB, 128) for m in range(2)], axis=1
        )
        out = jnp.dot(a_ref[...], pair, preferred_element_type=F32).astype(BF)
        for m in range(2):
            lo = (m * 2 + p) * 256
            o_ref[:, lo : lo + 128] = half_ref[p, hh, pr, :, m * 128 : (m + 1) * 128]
            o_ref[:, lo + 128 : lo + 256] = out[:, m * 128 : (m + 1) * 128]
    zl = lax.rem(lax.axis_index("island"), 4)

    @pl.when(step == 0)
    def _():
        for k in range(4):
            @pl.when(zl == k)
            def _():
                nbo_ref[...] = nb_ref[pl.ds(52 * k, 52), :]
                nmo_ref[...] = nm_ref[pl.ds(52 * k, 52), :]


def per_device(
    acts, grad_out, next_acts, inner_params, adam_first, adam_second, base_params, outer_moment
):
    n = len(CHUNKS)
    dma, vm = pltpu.SemaphoreType.DMA, pltpu.VMEM
    hbm = pl.BlockSpec(memory_space=pl.ANY)
    block = (NB, RB, 256)
    acts_tr = acts.T.reshape(NB, RB, 512)
    states = [a[0].T.reshape(block) for a in (inner_params, adam_first, adam_second)]
    states += [a.T.reshape(block) for a in (base_params, outer_moment)]
    w, nb, nm, na, half = pl.pallas_call(
        comm_kernel,
        out_shape=(
            vm((2, 2, 4) + block, BF), vm((RB, 256), F32), vm((RB, 256), F32), vm((512, 832), BF),
            vm((2, 2, 2, 512, 256), BF),
        ),
        in_specs=[hbm] * 8,
        out_specs=(pl.BlockSpec(memory_space=vm),) * 5,
        scratch_shapes=[
            vm((NB, RB, 512), BF), vm((4, 2, 2, 512, 256), BF), vm((4, 2) + block, BF), vm((4, 2) + block, BF),
            vm((4,) + block, F32),
            vm((2,) + block, BF), vm((2,) + block, BF), vm((2,) + block, BF), vm((2,) + block, BF),
            vm((2,) + block, BF), vm((2,) + block, BF), vm(block, BF), vm(block, BF), vm(block, F32),
            vm((3, RB, 256), F32), vm((8, RB, 256), BF),
            vm((5,) + block, F32), vm((832, 512), BF), vm((2, RB, 256), F32),
            dma((7,)), dma((4, 2, 2)), dma((4, 2, 2)), dma((4, 2, 2)), dma, dma, dma((n, 44)), dma((n, 44)),
        ],
        compiler_params=pltpu.CompilerParams(
            collective_id=0, has_side_effects=True, vmem_limit_bytes=48 * 2**20
        ),
        name="outer_round",
    )(acts_tr, grad_out, *states, next_acts.T)
    whole = pl.BlockSpec(memory_space=vm)
    small = pl.BlockSpec((52, 256), lambda i: (0, 0))
    next_out, base_out, moment_out = pl.pallas_call(
        project_kernel,
        grid=(4,),
        out_shape=(
            jax.ShapeDtypeStruct((512, 4096), BF),
            jax.ShapeDtypeStruct((52, 256), F32),
            jax.ShapeDtypeStruct((52, 256), F32),
        ),
        in_specs=[
            whole,
            whole,
            whole,
            whole,
            whole,
        ],
        out_specs=(pl.BlockSpec((512, 1024), lambda i: (0, i)), small, small),
        compiler_params=pltpu.CompilerParams(vmem_limit_bytes=24 * 2**20),
        name="project",
    )(na, w, nb, nm, half)
    return base_out.T, moment_out.T, next_out


def solution(mesh):
    in_specs = (
        P(("island", "fsdp"), None),
        P(("island", "fsdp"), None),
        P(("island", "fsdp"), None),
        P("island", "fsdp", None),
        P("island", "fsdp", None),
        P("island", "fsdp", None),
        P("fsdp", None),
        P("fsdp", None),
    )
    out_specs = (P("fsdp", "island"), P("fsdp", "island"), P(("island", "fsdp"), None))
    return jax.shard_map(
        per_device, mesh=mesh, in_specs=in_specs, out_specs=out_specs, check_vma=False
    )
```

time: 137 us -> 94.4 us (0.69)
  Pallas kernels: 136 us -> 93 us
    pallas_call x2, Pallas kernels: 136 us -> 93 us  [the longest x1 88.4 us: per_device(): pl.pallas_call(comm_kernel, out_shape=(vm((2, 2, 4) + block, BF), vm((RB,...]
where the time goes in v2:
time: 94.4 us; the launch traced here: 93.7 us
  Pallas kernels  93 us (99%)
    pallas_call x1, Pallas kernels, per_device(): pl.pallas_call(comm_kernel, out_shape=(vm((2, 2, 4) + block, BF), vm((RB,...  88.4 us
    pallas_call x1, Pallas kernels, per_device(): pl.pallas_call(project_kernel, grid=(4,), out_shape=(jax.ShapeDtypeStruct...  4.65 us

profile of v2, /device:TPU:1, one launch (start us, length us, event | category | flops | bytes accessed | tf_op | source)
XLA Modules:
  0.0 93.7 jit_solution(8858439784497422088)
XLA Ops:
  0.6 88.4 %outer_round.1 = (bf16[2,2,4,4,208,256]{5,4,3,2,1,0:T(8,128)(2,1)S(1)}, f32[208,256]{1,0:T(8,128)S(1)}, f32[208,256]{1,0:T(8,128)S(1)}, bf16[512,832]{1,0:T(8,128)(2,1)S(1)}, bf16[2,2,2,512,256]{4,3,2,1,0:T(8,128)(2,1)S(1)}) custom-call(bf16[4,208,512]{2,1,0:T(8,128)(2,1)} %bitcast.27, bf16[512,4096]{1,0:T(8,128)(2,1)} %gout.1, f32[4,208,256]{2,1,0:T(8,128)} %bitcast.28, ...), custom_call_target="tpu_custom_call" | custom-call | tf_op jit(solution)/shard_map/outer_round/pallas_call | solution.py:409
  89.0 4.7 %project.1 = (bf16[512,4096]{1,0:T(8,128)(2,1)}, f32[52,256]{1,0:T(8,128)}, f32[52,256]{1,0:T(8,128)}) custom-call(bf16[512,832]{1,0:T(8,128)(2,1)S(1)} %get-tuple-element.11.a_ref, bf16[2,2,4,4,208,256]{5,4,3,2,1,0:T(8,128)(2,1)S(1)} %get-tuple-element.12.w_ref, f32[208,256]{1,0:T(8,128)S(1)} %get-tuple-element.13.nb_ref, ...), custom_call_target="tpu_custom_call" | custom-call | tf_op jit(solution)/shard_map/project/pallas_call | solution.py:433

commit v3 on v2

--- a/solution.py
+++ b/solution.py
@@ -10,12 +10,12 @@
 BF = jnp.bfloat16
 F32 = jnp.float32
 CHUNKS = (
-    (0, 48, 0, 128), (48, 64, 0, 128), (112, 96, 0, 128), (0, 96, 128, 128), (96, 64, 128, 128), (160, 48, 128, 128)
+    (0, 48, 0, 128), (48, 64, 0, 128), (112, 96, 0, 128), (0, 64, 128, 128), (64, 64, 128, 128), (128, 48, 128, 128), (176, 32, 128, 128)
 )
-FIRST = (32, 32, 48, 48, 32, 32)
-WIDE = (4, 5)
+FIRST = (32, 32, 48, 32, 32, 32, 16)
+WIDE = (5, 6)
 DIRECT = (10, 9, 11, 6, 14, 2, 8, 5, 7, 13, 15, 1, 3, 4, 12)
-WIDE_ROWS, WIDE_LANES = pl.ds(96, 112), pl.ds(128, 128)
+WIDE_ROWS, WIDE_LANES = pl.ds(128, 80), pl.ds(128, 128)
 NB = 4
 RB = 208
 RELS = (2, 1, 3, 0)
@@ -290,7 +290,11 @@
         if k not in WIDE:
             live["core", k, 1].wait_recv()
 
-    def stage_mul():
+    def give(n, h):
+        give_mul(n, h)
+        give_send(n, h)
+
+    def mul_a():
         load_acts.wait()
         give_mul(0, 0)
         give_mul(0, 1)
@@ -300,32 +304,33 @@
         give_send(0, 0, 0)
         give_send(0, 1, 0)
         load_states()
-        give_mul(1, 1)
-        give_mul(2, 0)
-        keep(0, 0, s1.at[0], 0)
-        t1(0, (0,))
-        t1(1, (0,))
-        keep(0, 1, s1.at[1], 0)
-        t1(0, (1,))
-        t1(1, (1,))
+        give(1, 1)
+        give(2, 0)
+        for h in range(2):
+            keep(0, h, s1.at[h], 0)
+            for k in range(3):
+                t1(k, (h,))
+        give(1, 0)
+        give(2, 1)
         give_send(0, 0, 1)
         give_send(0, 1, 1)
-        give_send(1, 1)
-        give_send(2, 0)
-        give_mul(1, 0)
-        give_mul(2, 1)
         keep(1, 1, s2.at[1])
         keep(2, 0, s2.at[0])
         t2(0)
-        give_send(1, 0)
-        give_send(2, 1)
+        give(3, 0)
+        give(3, 1)
+
+    def mul_b():
+        keep(1, 0, part.at[0])
+        keep(2, 1, part.at[1])
+
+    def mul_c():
         keep(0, 0, s1.at[0], 1)
         keep(0, 1, s1.at[1], 1)
-        for n, h in ((3, 0), (3, 1)):
-            give_mul(n, h)
-            give_send(n, h)
-        for m, (n, h) in enumerate(((1, 0), (2, 1), (3, 0), (3, 1))):
-            keep(n, h, part.at[m])
+
+    def mul_d():
+        keep(3, 0, part.at[2])
+        keep(3, 1, part.at[3])
 
     def stage_rest():
         for cp in states:
@@ -355,16 +360,18 @@
             done.append(cp)
 
     steps = [
-        (stage_mul,), (t2, 1), (t3, 0), (t3, 1), (t1, 2), (t2, 2), (t4, 0), (t4, 1), (t3, 2), (t1, 3),
-        (stage_rest,), (t5, 0), (t2, 3), (t4, 2), (t5, 1), (t3, 3), (t6, 0), (t1, 5), (t2, 5), (t2, 4), (t6, 1),
-        (t4, 3), (t3, 5), (t1, 4), (t5, 2), (t7, 0), (drain, 40), (t4, 5), (t3, 4), (t7, 1), (t6, 2), (t5, 3),
-        (t7b, 0), (t4, 4), (gather_two, 0, 0), (t5, 5), (t7b, 1), (gather_two, 1, 0), (t6, 3), (t7, 2),
-        (drain, 40), (gather_two, 0, 1), (t6, 5), (gather_three, 0, 0), (t5, 4), (gather_two, 1, 1),
-        (gather_three, 1, 0), (t7, 3), (gather_two, 2, 0), (t6, 4), (t7b, 2), (gather_two, 3, 0), (t7, 5),
-        (drain, 60), (gather_three, 1, 1), (t7b, 3), (gather_two, 2, 1), (t7, 4), (drain, 60),
-        (gather_three, 0, 1), (gather_all, 5), (gather_two, 3, 1), (gather_three, 2, 1), (gather_three, 2, 0),
-        (t10, 1), (t10, 0), (gather_three, 3, 0), (gather_all, 4), (t10, 5), (t10, 2), (gather_three, 3, 1),
-        (product, 0, 1), (product, 1, 0), (product, 0, 0), (t10, 4), (product, 1, 1), (t10, 3),
+        (mul_a,), (mul_b,), (t3, 0), (t3, 1), (stage_rest,), (t2, 1), (t2, 2), (t3, 2), (mul_c,), (mul_d,),
+        (t4, 0), (t4, 1), (t1, 3), (t5, 0), (t1, 6), (t4, 2), (t2, 3), (t3, 3), (t1, 4), (t2, 4), (t5, 1),
+        (t6, 0), (t4, 3), (t3, 4), (t6, 1), (t5, 2), (t2, 6), (t7, 0), (drain, 40), (t1, 5), (t3, 6), (t2, 5),
+        (t4, 4), (t6, 2), (t3, 5), (t5, 3), (t7, 1), (t4, 6), (gather_two, 0, 0), (t5, 4), (t4, 5), (t7b, 0),
+        (gather_two, 1, 0), (t7, 2), (drain, 40), (t6, 3), (t7b, 1), (t5, 6), (gather_two, 0, 1), (t6, 4),
+        (t5, 5), (gather_two, 1, 1), (t6, 6), (t7b, 2), (gather_two, 2, 0), (t7, 3), (gather_three, 1, 0),
+        (t7, 4), (t6, 5), (gather_two, 2, 1), (gather_three, 0, 1), (t7, 6), (drain, 60), (gather_three, 0, 0),
+        (t7b, 3), (gather_two, 3, 0), (gather_three, 1, 1), (t7b, 4), (gather_two, 4, 0), (gather_three, 2, 1),
+        (gather_three, 2, 0), (t7, 5), (drain, 60), (gather_two, 4, 1), (t10, 0), (gather_three, 3, 0),
+        (gather_two, 3, 1), (t10, 1), (gather_all, 6), (t10, 6), (t10, 2), (gather_all, 5), (gather_three, 4, 1),
+        (gather_three, 4, 0), (gather_three, 3, 1), (product, 0, 0), (product, 0, 1), (product, 1, 0), (t10, 5),
+        (product, 1, 1), (t10, 3), (t10, 4),
     ]
     for step in steps:
         step[0](*step[1:])

time: 94.4 us -> 89.5 us (0.948)
  Pallas kernels: 93 us -> 88.3 us
    pallas_call x1, Pallas kernels: 88.4 us -> 83.6 us  [per_device(): pl.pallas_call(comm_kernel, out_shape=(vm((2, 2, 4) + block, BF), vm((RB,...]
where the time goes in v3:
time: 89.5 us; the launch traced here: 88.9 us
  Pallas kernels  88.3 us (99%)
    pallas_call x1, Pallas kernels, per_device(): pl.pallas_call(comm_kernel, out_shape=(vm((2, 2, 4) + block, BF), vm((RB,...  83.6 us
    pallas_call x1, Pallas kernels, per_device(): pl.pallas_call(project_kernel, grid=(4,), out_shape=(jax.ShapeDtypeStruct...  4.65 us

profile of v3, /device:TPU:1, one launch (start us, length us, event | category | flops | bytes accessed | tf_op | source)
XLA Modules:
  0.0 88.9 jit_solution(18064858819098043177)
XLA Ops:
  0.6 83.6 %outer_round.1 = (bf16[2,2,4,4,208,256]{5,4,3,2,1,0:T(8,128)(2,1)S(1)}, f32[208,256]{1,0:T(8,128)S(1)}, f32[208,256]{1,0:T(8,128)S(1)}, bf16[512,832]{1,0:T(8,128)(2,1)S(1)}, bf16[2,2,2,512,256]{4,3,2,1,0:T(8,128)(2,1)S(1)}) custom-call(bf16[4,208,512]{2,1,0:T(8,128)(2,1)} %bitcast.27, bf16[512,4096]{1,0:T(8,128)(2,1)} %gout.1, f32[4,208,256]{2,1,0:T(8,128)} %bitcast.28, ...), custom_call_target="tpu_custom_call" | custom-call | tf_op jit(solution)/shard_map/outer_round/pallas_call | solution.py:416
  84.2 4.7 %project.1 = (bf16[512,4096]{1,0:T(8,128)(2,1)}, f32[52,256]{1,0:T(8,128)}, f32[52,256]{1,0:T(8,128)}) custom-call(bf16[512,832]{1,0:T(8,128)(2,1)S(1)} %get-tuple-element.11.a_ref, bf16[2,2,4,4,208,256]{5,4,3,2,1,0:T(8,128)(2,1)S(1)} %get-tuple-element.12.w_ref, f32[208,256]{1,0:T(8,128)S(1)} %get-tuple-element.13.nb_ref, ...), custom_call_target="tpu_custom_call" | custom-call | tf_op jit(solution)/shard_map/project/pallas_call | solution.py:440
